TPU v7x, 512 devices: a whole 4x4x16 slice. The times are simulated.
512 devices in a mesh: section: 4 (over z_lo), group: 16 (over x, y), tensor: 8 (over z_hi, core).
Axes of the slice: x: 4, y: 4, z: 16 (z_hi: 4, z_lo: 4; z = z_hi * 4 + z_lo), core: 2. Of those that a mesh axis runs over, the one named last changes fastest.
Arguments:
- x_pre: bfloat16 [1024, 32, 8192], P(('section', 'group'), None, 'tensor'), may hold values from -6 to 6
- z_pre: bfloat16 [1024, 32, 8192], P(('section', 'group'), None, 'tensor'), may hold values from -6 to 6
- b_pre: bfloat16 [1024, 32, 16], P(('section', 'group')), may hold values from -4 to 4
- c_pre: bfloat16 [1024, 32, 16], P(('section', 'group')), may hold values from -4 to 4
- dt_pre: float32 [1024, 32, 128], P(('section', 'group'), None, 'tensor'), may hold values from -6 to 6
- lengths: int32 [1024], P(('section', 'group')), may hold values from 1 to 32, as said below
- owner: int32 [1024], replicated, may hold values from 0 to 15, as said below
- dec_x: bfloat16 [1024, 4, 8192], P(('section', 'group'), None, 'tensor'), may hold values from -6 to 6
- dec_z: bfloat16 [1024, 4, 8192], P(('section', 'group'), None, 'tensor'), may hold values from -6 to 6
- dec_b: bfloat16 [1024, 4, 16], P(('section', 'group')), may hold values from -4 to 4
- dec_c: bfloat16 [1024, 4, 16], P(('section', 'group')), may hold values from -4 to 4
- dec_dt: float32 [1024, 4, 128], P(('section', 'group'), None, 'tensor'), may hold values from -6 to 6
- decay_rate: float32 [128], P('tensor'), may hold values from 0.002 to 0.05
- dt_bias: float32 [128], P('tensor'), may hold values from -1 to 1
- skip: float32 [128], P('tensor'), may hold values from 0.5 to 1.5
- norm_gain: float32 [8192], P('tensor'), may hold values from 0.5 to 1.5
Outputs:
- pre_out: bfloat16 [1024, 32, 8192], P(('section', 'group'), None, 'tensor')
- dec_out: bfloat16 [1024, 4, 8192], P(('section', 'group'), None, 'tensor')
- dec_state: float32 [1024, 16, 8192], P(('section', 'group'), None, 'tensor')
Inputs may be any that keep to these rules, and one draw needn't show every extreme that they name: `lengths`: each request has 1 to 32 new tokens; in each aligned block of 16 requests (one cell) one request has exactly 32. owner[r] is the group, within the next pool along the section axis, of request r's decode owner. The 16 requests of one cell go exactly 2 each to half of the groups; each group of a pool receives exactly 16 requests from the previous pool.
All inputs are finite; a program needn't handle non-finite values.
Results may differ from a plain program's by a relative error of at most 0.0012.
Values sent between devices are 32-bit elements; how exact they have to be, the bound alone decides.
A program may use at most 64 MiB of HBM per device.

v0:
```python
import jax
import jax.numpy as jnp
from jax import lax
from jax.sharding import PartitionSpec as P

CHAN = 8192


EPS = 1e-05
HIGH = lax.Precision.HIGHEST


def from_behind(array, axis, by):
    size = lax.axis_size(axis)
    return lax.ppermute(array, axis, [(i, (i + by) % size) for i in range(size)])


def per_channel(values, head_size):
    return jnp.broadcast_to(values[..., None], values.shape + (head_size,)).reshape(
        values.shape[:-1] + (values.shape[-1] * head_size,)
    )


def local(
    x_pre,
    z_pre,
    b_pre,
    c_pre,
    dt_pre,
    lengths,
    owner,
    dec_x,
    dec_z,
    dec_b,
    dec_c,
    dec_dt,
    decay_rate,
    dt_bias,
    skip,
    norm_gain,
):
    req_count, tok_slots, channels = x_pre.shape
    head_count = dt_pre.shape[2]
    head_size = channels // head_count
    state_count = b_pre.shape[2]
    slot_count = dec_x.shape[0]
    step_count = dec_x.shape[1]
    group_count = lax.axis_size("group")
    sections = lax.axis_size("section")
    pair_cap = 2 * req_count // group_count
    me_section = lax.axis_index("section")
    me_group = lax.axis_index("group")
    cell_id = me_section * group_count + me_group
    positions = jnp.arange(tok_slots, dtype=jnp.int32)
    live_tokens = (positions[None, :] < lengths[:, None]).astype(jnp.float32)
    step_size = jax.nn.softplus(dt_pre + dt_bias) * live_tokens[:, :, None]
    log_cum = jnp.cumsum(-decay_rate * step_size, axis=1)
    b_float = b_pre.astype(jnp.float32)
    c_float = c_pre.astype(jnp.float32)
    gram_matrix = jnp.einsum("rtn,rsn->rts", c_float, b_float, precision=HIGH)
    causal = (positions[:, None] >= positions[None, :])[None, :, :, None]
    log_gap = log_cum[:, :, None, :] - log_cum[:, None, :, :]
    weights = jnp.where(causal, jnp.exp(jnp.where(causal, log_gap, 0.0)), 0.0)
    weights = weights * gram_matrix[:, :, :, None] * step_size[:, None, :, :]
    x_float = x_pre.astype(jnp.float32)
    x_heads = x_float.reshape(req_count, tok_slots, head_count, head_size)
    intra = jnp.einsum("rtsh,rshp->rthp", weights, x_heads, precision=HIGH).reshape(
        req_count, tok_slots, channels
    )
    carry_weight = jnp.exp(log_cum[:, -1:, :] - log_cum) * step_size
    weighted = x_heads * carry_weight[:, :, :, None]
    final_state = jnp.einsum("rsn,rshp->rnhp", b_float, weighted, precision=HIGH).reshape(
        req_count, state_count, channels
    )
    skip_chan = per_channel(skip, head_size)
    pre_gated = (intra + skip_chan * x_float) * jax.nn.silu(z_pre.astype(jnp.float32))
    pre_squares = jnp.sum(pre_gated * pre_gated, axis=2)
    pre_total = lax.psum(pre_squares, "tensor")
    pre_out = (
        pre_gated
        * lax.rsqrt(pre_total / CHAN + EPS)[:, :, None]
        * norm_gain
        * live_tokens[:, :, None]
    ).astype(jnp.bfloat16)
    owner_local = lax.dynamic_slice_in_dim(owner, cell_id * req_count, req_count)
    req_index = jnp.arange(req_count, dtype=jnp.int32)
    same_owner = owner_local[:, None] == owner_local[None, :]
    earlier = req_index[None, :] < req_index[:, None]
    pair_rank = jnp.sum((same_owner & earlier).astype(jnp.int32), axis=1)
    slot_index = owner_local * pair_cap + pair_rank
    slot_width = group_count * pair_cap
    select = slot_index[None, :] == jnp.arange(slot_width, dtype=jnp.int32)[:, None]
    source = jnp.sum(jnp.where(select, req_index[None, :], 0), axis=1)
    present = jnp.any(select, axis=1).astype(jnp.float32)
    send_buffer = (jnp.take(final_state, source, axis=0) * present[:, None, None]).reshape(
        group_count, pair_cap, state_count, channels
    )
    spread = lax.all_to_all(send_buffer, "group", split_axis=0, concat_axis=0, tiled=True)
    arrived = from_behind(spread, "section", 1)
    arrived = arrived.reshape(slot_width, state_count, channels)
    source_section = (me_section + sections - 1) % sections
    owner_rows = lax.dynamic_slice_in_dim(
        owner.reshape(-1, req_count), source_section * group_count, group_count, 0
    )
    sent_count = jnp.sum((owner_rows == me_group).astype(jnp.int32), axis=1)
    offsets = jnp.cumsum(sent_count) - sent_count
    slot_ids = jnp.arange(slot_count, dtype=jnp.int32)
    match = (offsets[None, :] <= slot_ids[:, None]) & (
        slot_ids[:, None] < (offsets + sent_count)[None, :]
    )
    row_of = (
        jnp.arange(group_count, dtype=jnp.int32)[None, :] * pair_cap
        + slot_ids[:, None]
        - offsets[None, :]
    )
    rows = jnp.sum(jnp.where(match, row_of, 0), axis=1)
    carry_state = jnp.take(arrived, rows, axis=0)
    outputs = []
    for step_index in range(step_count):
        dec_step = jax.nn.softplus(dec_dt[:, step_index] + dt_bias)
        decay_step = per_channel(jnp.exp(-decay_rate * dec_step), head_size)
        dec_float = dec_x[:, step_index].astype(jnp.float32)
        inject = per_channel(dec_step, head_size) * dec_float
        carry_state = (
            carry_state * decay_step[:, None, :]
            + dec_b[:, step_index].astype(jnp.float32)[:, :, None] * inject[:, None, :]
        )
        mixed = (
            jnp.sum(carry_state * dec_c[:, step_index].astype(jnp.float32)[:, :, None], axis=1)
            + skip_chan * dec_float
        )
        gated_out = mixed * jax.nn.silu(dec_z[:, step_index].astype(jnp.float32))
        squares = jnp.sum(gated_out * gated_out, axis=1)
        total = lax.psum(squares, "tensor")
        outputs.append(gated_out * lax.rsqrt(total / CHAN + EPS)[:, None] * norm_gain)
    dec_out = jnp.stack(outputs, axis=1).astype(jnp.bfloat16)
    return (pre_out, dec_out, carry_state)


def solution(mesh):
    return jax.shard_map(
        local,
        mesh=mesh,
        in_specs=(
            P(("section", "group"), None, "tensor"),
            P(("section", "group"), None, "tensor"),
            P(("section", "group"), None, None),
            P(("section", "group"), None, None),
            P(("section", "group"), None, "tensor"),
            P(("section", "group")),
            P(),
            P(("section", "group"), None, "tensor"),
            P(("section", "group"), None, "tensor"),
            P(("section", "group"), None, None),
            P(("section", "group"), None, None),
            P(("section", "group"), None, "tensor"),
            P("tensor"),
            P("tensor"),
            P("tensor"),
            P("tensor"),
        ),
        out_specs=(
            P(("section", "group"), None, "tensor"),
            P(("section", "group"), None, "tensor"),
            P(("section", "group"), None, "tensor"),
        ),
        check_vma=False,
    )
```

profile of v0, /device:TPU:1, one launch (start us, length us, event | category | flops | bytes accessed | tf_op | source)
XLA Modules:
  0.0 158.6 jit_solution(8210618663187005559)
XLA Ops:
  0.7 0.8 dynamic_slice.7
  1.4 0.2 convert_reduce_fusion
  1.6 0.8 multiply_add_fusion.4
  2.7 1.1 copy.77
  3.7 0.7 fusion.105
  4.4 0.7 neg.81
  5.1 4.1 %reshape.506 = f32[16,32,16,64]{3,2,1,0:T(8,128)} reshape(bf16[16,32,1024]{2,1,0:T(8,128)(2,1)} %param.16) | data formatting | bytes 3145728 | tf_op jit(solution)/shard_map/reshape | solution.py:66
  9.2 0.2 fusion.24
  9.4 0.7 copy-done.3
  10.1 0.2 exponential_multiply_fusion
  10.5 4.9 %fusion.23 = f32[16,16,16,64]{3,1,2,0:T(8,128)S(1)} fusion(f32[16,32,16,64]{3,2,1,0:T(8,128)} %reshape.506, f32[16,32,16]{1,2,0:T(8,128)S(1)} %copy.85, bf16[16,32,16]{1,2,0:T(8,128)(2,1)S(1)} %copy-done), kind=kOutput, calls=%fused_computation.29 | convolution fusion | flops 101187584 | bytes 3194880 | tf_op jit(solution)/shard_map/rsn,rshp->rnhp/dot_general | solution.py:72
  15.4 0.7 copy.87
  16.0 0.6 reshape.507
  16.7 0.7 gather_fusion
  17.4 1.6 %select_multiply_fusion = f32[16,2,16,1024]{3,2,1,0:T(8,128)} fusion(f32[16,2,16,1024]{3,2,1,0:T(8,128)S(1)} %bitcast.182, f32[16,2]{1,0:T(8,128)S(1)} %reshape.513, pred[16,2]{1,0:T(8,128)(4,1)S(1)} %compare_and_fusion), kind=kLoop, calls=%fused_computation.19 | loop fusion | flops 1048576 | bytes 4194464 | tf_op jit(solution)/shard_map/mul | solution.py:95
  19.1 7.8 %all-to-all-start = ((f32[16,2,16,1024]{3,2,1,0:T(8,128)}), f32[16,2,16,1024]{3,2,1,0:T(8,128)}, u32[]{:S(2)}, u32[]{:S(2)}) async-start(f32[16,2,16,1024]{3,2,1,0:T(8,128)} %select_multiply_fusion), calls=%async_computation | async-start | bytes 4194304 | tf_op jit(solution)/shard_map/all_to_all | solution.py:98
  26.9 2.4 %reshape.501 = bf16[16,32,16,64]{3,2,1,0:T(8,128)(2,1)} reshape(bf16[16,32,1024]{2,1,0:T(8,128)(2,1)S(1)} %copy-done.1) | data formatting | bytes 2097152 | tf_op jit(solution)/shard_map/reshape | solution.py:66
  29.8 0.2 fusion.116
  30.0 5.1 %fusion.8 = f32[16,32,16,64]{3,1,2,0:T(8,128)S(1)} fusion(bf16[16,32,16,64]{3,2,1,0:T(8,128)(2,1)} %reshape.501, f32[16,32,16]{1,2,0:T(8,128)S(1)} %copy.80, f32[16,32,32]{2,1,0:T(8,128)S(1)} %fusion.116, f32[16,32,16]{1,2,0:T(8,128)S(1)} %copy.78, pred[32,32]{1,0:T(8,128)(4,1)S(1)} %iota_compare_fusion.1), kind=kOutput, calls=%fused_computation.13 | convolution fusion | flops 202637312 | bytes 3277824 | tf_op jit(solution)/shard_map/rtsh,rshp->rthp/dot_general | solution.py:67
  35.1 5.2 %copy.82 = f32[16,32,16,64]{3,2,1,0:T(8,128)} copy(f32[16,32,16,64]{3,1,2,0:T(8,128)S(1)} %fusion.8) | data formatting | bytes 4194304 | tf_op jit(solution)/shard_map/rtsh,rshp->rthp/transpose | solution.py:67
  40.3 3.5 %reshape.502 = f32[16,32,1024]{2,1,0:T(8,128)S(1)} reshape(f32[16,32,16,64]{3,2,1,0:T(8,128)} %copy.82) | data formatting | bytes 4194304 | tf_op jit(solution)/shard_map/reshape | solution.py:67
  44.3 0.7 reshape.512
  45.2 0.7 mul.571
  46.0 0.7 mul.550
  46.8 0.7 reshape.509
  47.6 0.7 reshape.510
  48.4 0.7 mul.529
  49.3 0.7 mul.505
  50.5 1.4 all-to-all-done
  51.9 6.5 %collective-permute-start = (f32[16,2,16,1024]{3,2,1,0:T(8,128)}, f32[16,2,16,1024]{3,2,1,0:T(8,128)S(1)}, u32[]{:S(2)}, u32[]{:S(2)}) collective-permute-start(f32[16,2,16,1024]{3,2,1,0:T(8,128)} %all-to-all-done), channel_id=1, source_target_pairs={{0,128},{128,256},{256,384},{384,0},{1,129},{129,257},{257,385},{3... | collective-permute-start | bytes 6291464 | tf_op jit(solution)/shard_map/ppermute | solution.py:15
  58.4 0.5 compare_and_fusion.1
  59.0 0.6 slice_convert_fusion
  59.6 0.6 slice_convert_fusion.1
  60.2 1.4 fusion.113
  61.7 1.5 fusion.78
  63.2 1.6 fusion.56
  64.7 2.1 %fusion.114 = (bf16[16,1,1024]{2,1,0:T(2,128)(2,1)}, bf16[16,1,1024]{2,1,0:T(2,128)(2,1)}, bf16[16,1,1024]{2,1,0:T(2,128)(2,1)}, bf16[16,1,1024]{2,1,0:T(2,128)(2,1)}) fusion(bf16[16,4,1024]{2,1,0:T(4,128)(2,1)} %param.24), kind=kLoop, calls=%fused_computation.197 | loop fusion | bytes 262144 | tf_op jit(solution)/shard_map/slice | solution.py:132
  66.9 2.8 %multiply_reduce_fusion = (f32[16,32]{1,0:T(8,128)}, f32[16,32,1024]{2,1,0:T(8,128)}) fusion(bf16[16,32,1024]{2,1,0:T(8,128)(2,1)S(1)} %copy-done.5, f32[16,32,1024]{2,1,0:T(8,128)S(1)} %reshape.502, bf16[16,32,1024]{2,1,0:T(8,128)(2,1)S(1)} %copy-done.1, f32[1024]{0:T(1024)S(1)} %mul.481), kind=kLoop, calls=%fused_computation.22 | loop fusion | flops 5766656 | bytes 6297600 | tf_op jit(solution)/shard_map/reduce_sum | solution.py:77
  69.6 34.0 %collective-permute-done = f32[16,2,16,1024]{3,2,1,0:T(8,128)S(1)} collective-permute-done((f32[16,2,16,1024]{3,2,1,0:T(8,128)}, f32[16,2,16,1024]{3,2,1,0:T(8,128)S(1)}, u32[]{:S(2)}, u32[]{:S(2)}) %collective-permute-start) | collective-permute-done | bytes 2097184 | tf_op jit(solution)/shard_map/ppermute | solution.py:15
  103.7 1.3 copy-done.12
  105.0 2.2 %gather_fusion.1 = f32[16,16,1024]{2,1,0:T(8,128)S(1)} fusion(f32[32,16,1024]{2,1,0:T(8,128)} %bitcast.183, s32[1024]{0:T(1024)S(1)} %pad_clamp_fusion), kind=kCustom, calls=%fused_computation.1 | custom fusion | bytes 2097216 | tf_op jit(solution)/shard_map/jit(_take)/gather | solution.py:117
  107.3 3.9 %multiply_reduce_fusion.1 = (f32[16,1024]{1,0:T(8,128)S(1)}, f32[16,16,1024]{2,1,0:T(8,128)}, f32[16,1024]{1,0:T(8,128)}, f32[16,1024]{1,0:T(8,128)S(1)}, f32[16,1024]{1,0:T(8,128)S(1)}) fusion(f32[16,16]{1,0:T(8,128)} %bitcast.184, f32[16,1024]{1,0:T(8,128)} %get-tuple-element.69, f32[16,16]{1,0:T(8,128)} %bitcast.188, f32[16,1024]{1,0:T(8,128)} %mul.571, ...), kind=kLoop, calls=%fused_computation.30 | loop fusion | flops 5439488 | bytes 2891792 | tf_op jit(solution)/shard_map/reduce_sum | solution.py:129
  111.2 0.6 copy-done.6
  111.8 1.1 fusion.101
  113.0 42.3 %all-reduce = (f32[16,32]{1,0:T(8,128)S(1)}, f32[16]{0:T(128)S(1)}, f32[16]{0:T(128)S(1)}, f32[16]{0:T(128)S(1)}, f32[16]{0:T(128)S(1)}) all-reduce(f32[16,32]{1,0:T(8,128)} %get-tuple-element.31, f32[16]{0:T(128)S(1)} %get-tuple-element.15, ...), channel_id=1, replica_groups=mesh['section'=4,'group'=16,'tensor'=8] {'tensor'}, use_global_device_ids=true, to_apply=%region_2.3 | all-reduce | flops 576 | bytes 4608 | tf_op jit(solution)/shard_map/psum | solution.py:78
  155.3 1.2 fusion.61
  156.6 0.8 copy.99
  157.3 1.3 multiply_convert_fusion
  (83 shorter events, 2.7 us)
Async XLA Ops:
  0.6 9.9 %copy-start = (bf16[16,32,16]{1,2,0:T(8,128)(2,1)S(1)}, bf16[16,32,16]{1,2,0:T(8,128)(2,1)}, u32[]{:S(2)}) copy-start(bf16[16,32,16]{1,2,0:T(8,128)(2,1)} %param.18) | copy-start | bytes 49156
  5.1 4.1 %copy-start.19 = (f32[16]{0:T(128)S(1)}, f32[16]{0:T(128)}, u32[]{:S(2)}) copy-start(f32[16]{0:T(128)} %param.29) | copy-start | bytes 196
  9.4 0.7 copy-start.3
  19.1 7.8 %copy-start.1 = (bf16[16,32,1024]{2,1,0:T(8,128)(2,1)S(1)}, bf16[16,32,1024]{2,1,0:T(8,128)(2,1)}, u32[]{:S(2)}) copy-start(bf16[16,32,1024]{2,1,0:T(8,128)(2,1)} %param.16) | copy-start | bytes 3145732
  19.1 32.9 %all-to-all-start = ((f32[16,2,16,1024]{3,2,1,0:T(8,128)}), f32[16,2,16,1024]{3,2,1,0:T(8,128)}, u32[]{:S(2)}, u32[]{:S(2)}) async-start(f32[16,2,16,1024]{3,2,1,0:T(8,128)} %select_multiply_fusion), calls=%async_computation | async-start | bytes 4194304 | tf_op jit(solution)/shard_map/all_to_all | solution.py:98
  26.9 2.4 %copy-start.4 = (f32[16,32,16]{2,0,1:T(8,128)S(1)}, f32[16,32,16]{2,0,1:T(8,128)}, u32[]{:S(2)}) copy-start(f32[16,32,16]{2,0,1:T(8,128)} %copy-done.3) | copy-start | bytes 98308
  26.9 2.8 %copy-start.18 = (s32[1024]{0:T(1024)S(1)}, s32[1024]{0:T(1024)}, u32[]{:S(2)}) copy-start(s32[1024]{0:T(1024)} %param.22) | copy-start | bytes 12292
  26.9 2.9 %copy-start.15 = (bf16[16,32,16]{1,2,0:T(8,128)(2,1)S(1)}, bf16[16,32,16]{1,2,0:T(8,128)(2,1)}, u32[]{:S(2)}) copy-start(bf16[16,32,16]{1,2,0:T(8,128)(2,1)} %param.19) | copy-start | bytes 49156
  40.3 3.5 %copy-start.20 = (f32[16]{0:T(128)S(1)}, f32[16]{0:T(128)}, u32[]{:S(2)}) copy-start(f32[16]{0:T(128)} %param.30) | copy-start | bytes 196
  40.3 3.7 %copy-start.16 = (f32[16,4,16]{2,1,0:T(4,128)S(1)}, f32[16,4,16]{2,1,0:T(4,128)}, u32[]{:S(2)}) copy-start(f32[16,4,16]{2,1,0:T(4,128)} %param.27) | copy-start | bytes 12292
  43.8 15.2 %copy-start.13 = (bf16[16,4,16]{2,1,0:T(4,128)(2,1)S(1)}, bf16[16,4,16]{2,1,0:T(4,128)(2,1)}, u32[]{:S(2)}) copy-start(bf16[16,4,16]{2,1,0:T(4,128)(2,1)} %param.26) | copy-start | bytes 6148
  43.8 15.8 %copy-start.14 = (bf16[16,4,16]{2,1,0:T(4,128)(2,1)S(1)}, bf16[16,4,16]{2,1,0:T(4,128)(2,1)}, u32[]{:S(2)}) copy-start(bf16[16,4,16]{2,1,0:T(4,128)(2,1)} %param.25) | copy-start | bytes 6148
  51.9 14.9 %copy-start.5 = (bf16[16,32,1024]{2,1,0:T(8,128)(2,1)S(1)}, bf16[16,32,1024]{2,1,0:T(8,128)(2,1)}, u32[]{:S(2)}) copy-start(bf16[16,32,1024]{2,1,0:T(8,128)(2,1)} %param.17) | copy-start | bytes 3145732
  51.9 51.7 %collective-permute-start = (f32[16,2,16,1024]{3,2,1,0:T(8,128)}, f32[16,2,16,1024]{3,2,1,0:T(8,128)S(1)}, u32[]{:S(2)}, u32[]{:S(2)}) collective-permute-start(f32[16,2,16,1024]{3,2,1,0:T(8,128)} %all-to-all-done), channel_id=1, source_target_pairs={{0,128},{128,256},{256,384},{384,0},{1,129},{129,257},{257,385},{3... | collective-permute-start | bytes 6291464 | tf_op jit(solution)/shard_map/ppermute | solution.py:15
  103.7 1.3 copy-start.12
  107.2 4.6 %copy-start.8 = (bf16[16,1,1024]{2,1,0:T(2,128)(2,1)S(1)}, bf16[16,1,1024]{2,1,0:T(2,128)(2,1)}, u32[]{:S(2)}) copy-start(bf16[16,1,1024]{2,1,0:T(2,128)(2,1)} %get-tuple-element.40) | copy-start | bytes 98308
  107.2 4.6 %copy-start.9 = (bf16[16,1,1024]{2,1,0:T(2,128)(2,1)S(1)}, bf16[16,1,1024]{2,1,0:T(2,128)(2,1)}, u32[]{:S(2)}) copy-start(bf16[16,1,1024]{2,1,0:T(2,128)(2,1)} %get-tuple-element.41) | copy-start | bytes 98308
  107.2 4.6 %copy-start.10 = (bf16[16,1,1024]{2,1,0:T(2,128)(2,1)S(1)}, bf16[16,1,1024]{2,1,0:T(2,128)(2,1)}, u32[]{:S(2)}) copy-start(bf16[16,1,1024]{2,1,0:T(2,128)(2,1)} %get-tuple-element.42) | copy-start | bytes 98308
  107.2 4.6 %copy-start.11 = (bf16[16,1,1024]{2,1,0:T(2,128)(2,1)S(1)}, bf16[16,1,1024]{2,1,0:T(2,128)(2,1)}, u32[]{:S(2)}) copy-start(bf16[16,1,1024]{2,1,0:T(2,128)(2,1)} %get-tuple-element.43) | copy-start | bytes 98308
  107.2 48.1 %copy-start.17 = (f32[1024]{0:T(1024)S(1)}, f32[1024]{0:T(1024)}, u32[]{:S(2)}) copy-start(f32[1024]{0:T(1024)} %param.31) | copy-start | bytes 12292
  107.2 50.1 %copy-start.2 = (f32[16,32,1024]{2,1,0:T(8,128)S(1)}, f32[16,32,1024]{2,1,0:T(8,128)}, u32[]{:S(2)}) copy-start(f32[16,32,1024]{2,1,0:T(8,128)} %get-tuple-element.32) | copy-start | bytes 6291460
  111.2 0.6 copy-start.6
  111.2 1.8 %copy-start.7 = (f32[16,1024]{1,0:T(8,128)}, f32[16,1024]{1,0:T(8,128)S(1)}, u32[]{:S(2)}) copy-start(f32[16,1024]{1,0:T(8,128)S(1)} %get-tuple-element.35) | copy-start | bytes 196612
where the time goes:
time: 160 us; the launch traced here: 159 us
  blocking collectives  42.3 us (26%)
  waiting for transfers between devices  35.5 us (22%)
  local copies, waits for them, and re-layouts  35.1 us (22%)
  other arithmetic  20.2 us (13%)
  starting transfers between devices  14.3 us (9%)
  matrix products  10.2 us (6%)
    psum x1, blocking collectives, local(): pre_total = lax.psum(pre_squares, 'tensor')  42.3 us
    ppermute x1, waiting for transfers between devices, from_behind(): lax.ppermute(array, axis, [(i, (i + by) % size) for i in range(size)])  34 us
    all_to_all x1, starting transfers between devices, local(): lax.all_to_all(send_buffer, 'group', split_axis=0, concat_axis=0, tiled=T...  7.78 us
    ppermute x1, starting transfers between devices, from_behind(): lax.ppermute(array, axis, [(i, (i + by) % size) for i in range(size)])  6.5 us
    reshape x2, local copies, waits for them, and re-layouts, local(): x_heads = x_float.reshape(req_count, tok_slots, head_count, head_size)  6.48 us
    transpose x1, local copies, waits for them, and re-layouts, local(): jnp.einsum('rtsh,rshp->rthp', weights, x_heads, precision=HIGH)  5.18 us
    dot_general x1, matrix products, local(): jnp.einsum('rtsh,rshp->rthp', weights, x_heads, precision=HIGH)  5.08 us
    dot_general x1, matrix products, local(): jnp.einsum('rsn,rshp->rnhp', b_float, weighted, precision=HIGH)  4.87 us
  transfers between devices with their start and end apart: 2, of which 2 were waited for; matrix products, arithmetic and copies ran while one was open for 22% of the time, Pallas kernels for 0%

commit v1 on v0

v1 whole, which is shorter than its diff:
```python
import functools

import jax
import jax.numpy as jnp
from jax import lax
from jax.experimental import pallas as pl
from jax.experimental.pallas import tpu as pltpu
from jax.sharding import PartitionSpec as P

CHAN = 8192
EPS = 1e-05
MESH = pl.DeviceIdType.MESH
F32 = jnp.float32
BF16 = jnp.bfloat16

REQ = 16
LEN = 32
STATE = 16
HEADS = 16
WIDTH = 1024
STEPS = 4
SIDE = 4
GROUPS = 16
SECTIONS = 4
TENSORS = 8
PARTS = 8
PART = WIDTH // PARTS
BLOCK = 256


def iota(shape, dim):
    return lax.broadcasted_iota(jnp.int32, shape, dim)


def softplus(v):
    return jnp.maximum(v, 0.0) + jnp.log1p(jnp.exp(-jnp.abs(v)))


def silu(v):
    return v / (1.0 + jnp.exp(-v))


def two_terms(v):
    high = v.astype(BF16)
    return high, (v - high.astype(F32)).astype(BF16)


def three_terms(v):
    high = v.astype(BF16)
    rest = v - high.astype(F32)
    mid = rest.astype(BF16)
    return high, mid, (rest - mid.astype(F32)).astype(BF16)


def dot(a, b):
    return jnp.dot(a, b, preferred_element_type=F32)


def from_scalars(ref, where_index, count):
    acc = jnp.zeros(where_index.shape, ref.dtype)
    for k in range(count):
        acc = jnp.where(where_index == k, ref[k], acc)
    return acc


def kernel(
    lengths, owner, rate, bias, skip,
    b_t, c_t, dt_t, dec_x, dec_z, dec_b, dec_c, dec_dt, gain,
    x_hbm, z_hbm,
    pre_hbm, dec_hbm, state_hbm,
    *scratch,
):
    (x_v, z_v, turn, lhs, expand_lhs, mixed, squares, z_send, x_send, staged, pre_v,
     dec_v, dec_decay, dec_inject, dec_skip, dec_gate, dec_cols, dec_gated, dec_squares,
     pack, got, source, rows, local_sem, z_sem, x_sem, t_sem) = scratch[:27]
    z_recv = scratch[27:27 + PARTS]
    x_recv = scratch[27 + PARTS:27 + 2 * PARTS]

    section = lax.axis_index("section")
    group = lax.axis_index("group")
    tensor = lax.axis_index("tensor")
    gx, gy = group // SIDE, lax.rem(group, SIDE)
    ahead = lax.rem(section + 1, SECTIONS)
    behind = lax.rem(section + SECTIONS - 1, SECTIONS)

    def group_at(d):
        return lax.rem(gx + d // SIDE, SIDE) * SIDE + lax.rem(gy + lax.rem(d, SIDE), SIDE)

    blocks = WIDTH // BLOCK
    x_copies = []
    for k in range(blocks):
        cols = pl.ds(k * BLOCK, BLOCK)
        copy = pltpu.make_async_copy(x_hbm.at[:, :, cols], x_v.at[:, :, cols], local_sem.at[k])
        copy.start()
        x_copies.append(copy)
    z_copy = pltpu.make_async_copy(z_hbm, z_v, local_sem.at[blocks])
    z_copy.start()

    barrier = pltpu.get_barrier_semaphore()
    for to in (ahead, behind):
        pl.semaphore_signal(barrier, inc=1, device_id=(to, group, tensor), device_id_type=MESH)
    for d in range(1, GROUPS):
        pl.semaphore_signal(barrier, inc=1, device_id=(section, group_at(d), tensor), device_id_type=MESH)
    for d in range(1, TENSORS):
        pl.semaphore_signal(
            barrier, inc=1, device_id=(section, group, lax.rem(tensor + d, TENSORS)), device_id_type=MESH
        )

    turn[...] = jnp.zeros_like(turn)
    turn[:, 0:LEN] = dt_t[...].reshape(REQ * HEADS, LEN)
    logits = jnp.transpose(turn[...])[0:LEN]
    lane = iota((1, REQ * HEADS), 1)
    head_of, req_of = lax.rem(lane, HEADS), lane // HEADS
    live = iota((LEN, REQ * HEADS), 0) < from_scalars(lengths, req_of, REQ)
    step = jnp.where(live, softplus(logits + from_scalars(bias, head_of, HEADS)), 0.0)
    fall = from_scalars(rate, head_of, HEADS) * step
    lower = (iota((LEN, LEN), 0) >= iota((LEN, LEN), 1)).astype(F32).astype(BF16)
    total = sum(dot(lower, term) for term in three_terms(fall))
    shrink = jnp.exp(-total)
    grow = jnp.exp(total) * step

    turn[:, 0:LEN] = c_t[...].reshape(REQ * STATE, LEN).astype(F32)
    c_tok = jnp.transpose(turn[...])[0:LEN]
    spread = (lax.rem(iota((LEN, 3 * LEN), 1), LEN) == iota((LEN, 3 * LEN), 0)).astype(F32).astype(BF16)
    b_rep = dot(b_t[...].reshape(REQ * STATE, LEN), spread)
    lane3 = iota((LEN, 3 * LEN), 1)
    middle = (lane3 >= LEN) & (lane3 < 2 * LEN)
    causal = iota((LEN, 3 * LEN), 0) >= lax.rem(lane3, LEN)
    lane128 = iota((LEN, 128), 1) // HEADS
    half_reqs = 128 // HEADS
    for r in range(REQ):
        half = slice((r // half_reqs) * 128, (r // half_reqs) * 128 + 128)
        mine = lane128 == r % half_reqs
        for at, values in ((0, grow), (LEN, shrink)):
            high, low = two_terms(jnp.where(mine, values[:, half], 0.0))
            expand_lhs[r, at:at + LEN, 0:128] = high
            expand_lhs[r, at:at + LEN, 128:256] = low
        gram = dot(jnp.where(mine, c_tok[:, half], 0.0).astype(BF16), b_rep[half].astype(BF16))
        high = gram.astype(BF16).astype(F32)
        lhs[r, 0:LEN, :] = jnp.where(causal, jnp.where(middle, gram - high, high), 0.0).astype(BF16)
        lhs[r, LEN:LEN + STATE, :] = jnp.where(
            middle[0:STATE], 0.0, b_rep[r * STATE:(r + 1) * STATE]
        ).astype(BF16)

    z_out = []
    for k in range(blocks):
        x_copies[k].wait()
        cols = slice(k * BLOCK, (k + 1) * BLOCK)
        head_rows = lax.rem(iota((256, BLOCK), 0), HEADS)
        head_cols = iota((256, BLOCK), 1) // 64 + k * (BLOCK // 64)
        expand = (head_rows == head_cols).astype(F32).astype(BF16)
        skip_row = from_scalars(skip, iota((1, BLOCK), 1) // 64 + k * (BLOCK // 64), HEADS)

        def prefill(i, _, k=k, cols=cols, expand=expand, skip_row=skip_row):
            for sub in range(4):
                r = i * 4 + sub
                wide = dot(expand_lhs[r], expand)
                x_f = x_v[r, :, cols].astype(F32)
                high, low = two_terms(x_f * wide[0:LEN])
                res = dot(lhs[r], jnp.concatenate([high, high, low], axis=0))
                mixed[r, :, cols] = res[0:LEN] * wide[LEN:2 * LEN] + skip_row * x_f
                final = res[LEN:LEN + STATE] * wide[2 * LEN - 1:2 * LEN]
                for p in range(BLOCK // PART):
                    z_send[k * (BLOCK // PART) + p, r] = final[:, p * PART:(p + 1) * PART]
            return 0

        lax.fori_loop(0, REQ // 4, prefill, 0)
        if k == 0:
            pl.semaphore_wait(barrier, 2 + (GROUPS - 1) + (TENSORS - 1))
        for p in range(BLOCK // PART):
            j = k * (BLOCK // PART) + p
            copy = pltpu.make_async_remote_copy(
                z_send.at[j], z_recv[j], z_sem.at[0, j], z_sem.at[1, j],
                device_id=(ahead, group, tensor), device_id_type=MESH,
            )
            copy.start()
            z_out.append(copy)

    z_copy.wait()

    def gate(r, _):
        value = mixed[r] * silu(z_v[r].astype(F32))
        mixed[r] = value
        acc = jnp.zeros((LEN, 128), F32)
        for p in range(WIDTH // 128):
            part = value[:, p * 128:(p + 1) * 128]
            acc = acc + part * part
        squares[pl.ds(pl.multiple_of(r * LEN, LEN), LEN), :] = acc
        return 0

    lax.fori_loop(0, REQ, gate, 0)

    def exchange(which):
        copies = []
        for d in range(1, TENSORS):
            copy = pltpu.make_async_remote_copy(
                pack.at[which], got.at[which, d], t_sem.at[2 * which, d], t_sem.at[2 * which + 1, d],
                device_id=(section, group, lax.rem(tensor + d, TENSORS)), device_id_type=MESH,
            )
            copy.start()
            copies.append(copy)
        return copies

    pack[...] = jnp.zeros_like(pack)
    row8 = iota((8, 128), 0)
    packed = jnp.zeros((8, 128), F32)
    for q in range(4):
        sums = jnp.sum(jnp.transpose(squares[q * 128:(q + 1) * 128, :]), axis=0, keepdims=True)
        packed = jnp.where(row8 == q, sums, packed)
    pack[0] = packed
    pre_copies = exchange(0)

    turn[...] = jnp.zeros_like(turn)
    for s in range(REQ):
        turn[s * STEPS:(s + 1) * STEPS, 0:HEADS] = dec_dt[s]
    lane_d = iota((1, 128), 1)
    dec_step = softplus(turn[0:REQ * STEPS, :] + from_scalars(bias, lane_d, HEADS))
    dec_dec = jnp.exp(-from_scalars(rate, lane_d, HEADS) * dec_step)
    both = jnp.concatenate([dec_step, dec_dec], axis=0)
    heads_wide = (iota((128, WIDTH), 0) == iota((128, WIDTH), 1) // 64).astype(F32).astype(BF16)
    wide = sum(dot(term, heads_wide) for term in three_terms(both))
    pairs = REQ // 2
    dec_inject[...] = wide[0:REQ * STEPS].reshape(pairs, 8, WIDTH)
    dec_decay[...] = wide[REQ * STEPS:2 * REQ * STEPS].reshape(pairs, 8, WIDTH)
    skip_wide = from_scalars(skip, iota((1, WIDTH), 1) // 64, HEADS)
    for s in range(REQ):
        at = slice((s % 2) * STEPS, (s % 2) * STEPS + STEPS)
        x_f = dec_x[s].astype(F32)
        dec_inject[s // 2, at, :] = dec_inject[s // 2, at, :] * x_f
        dec_skip[s // 2, at, :] = skip_wide * x_f
        dec_gate[s // 2, at, :] = silu(dec_z[s].astype(F32))
    turn[...] = jnp.zeros_like(turn)
    for s in range(REQ):
        turn[s * STEPS:(s + 1) * STEPS, 0:STATE] = dec_b[s].astype(F32)
        turn[s * STEPS:(s + 1) * STEPS, STATE:2 * STATE] = dec_c[s].astype(F32)
    cols_t = jnp.transpose(turn[0:128, :])[0:2 * STATE]
    pick = (lax.rem(iota((128, WIDTH), 0), 8) == iota((128, WIDTH), 1) // 128).astype(F32).astype(BF16)
    lane_p = iota((2 * STATE, 128), 1) // 8

    for p in range(pairs):
        dec_cols[p] = dot(jnp.where(lane_p == p, cols_t, 0.0).astype(BF16), pick)
    dec_squares[...] = jnp.zeros_like(dec_squares)

    first_request = (behind * GROUPS + group) * REQ

    def find_source(h, _):
        low, high = jnp.int32(REQ - 1), jnp.int32(0)
        for r in range(REQ):
            is_it = owner[first_request + r] == h
            low = jnp.minimum(low, jnp.where(is_it, r, REQ - 1))
            high = jnp.maximum(high, jnp.where(is_it, r, 0))
        source[2 * h] = low
        source[2 * h + 1] = high
        return 0

    lax.fori_loop(0, GROUPS, find_source, 0)

    def find_rows(cell, carry):
        place, found = carry[0], carry[1:]
        count = jnp.int32(0)
        for r in range(REQ):
            count = count + jnp.where(owner[(behind * GROUPS + cell) * REQ + r] == group, 1, 0)
        has = jnp.where(count > 0, 1, 0)
        spot = jnp.where(count > 0, place, -1)
        return (place + has,) + tuple(jnp.where(spot == j, cell, v) for j, v in enumerate(found))

    found = lax.fori_loop(0, GROUPS, find_rows, (jnp.int32(0),) * (1 + REQ // 2))[1:]
    for j, cell in enumerate(found):
        rows[2 * j] = 2 * cell
        rows[2 * j + 1] = 2 * cell + 1

    def group_copy(j, d, count=1):
        rows_of = 2 * count
        return pltpu.make_async_remote_copy(
            x_send.at[j, pl.ds(2 * d, rows_of)],
            x_recv[j].at[pl.ds(2 * group if count == 1 else 2 * d, rows_of)],
            x_sem.at[0, j], x_sem.at[1, j],
            device_id=(section, group_at(d), tensor), device_id_type=MESH,
        )

    def forward(j):
        z_out[j].wait_recv()

        for p in range(2):
            x_recv[j][2 * group + p] = z_recv[j][source[2 * group + p]]

        def fill(d, _):
            h = group_at(d)
            for p in range(2):
                x_send[j, 2 * d + p] = z_recv[j][source[2 * h + p]]
            group_copy(j, d).start()
            return 0

        lax.fori_loop(1, GROUPS, fill, 0)

    state_out = []

    def decode(j):
        group_copy(j, 1, GROUPS - 1).wait_recv()
        cols = slice(j * PART, (j + 1) * PART)

        def pair(p, _):
            y = jnp.zeros((8, PART), F32)
            for i in range(2):
                state = x_recv[j][rows[2 * p + i]]
                for t in range(STEPS):
                    q = i * STEPS + t
                    b_col = dec_cols[p, 0:STATE, q * 128:(q + 1) * 128]
                    c_col = dec_cols[p, STATE:2 * STATE, q * 128:(q + 1) * 128]
                    state = state * dec_decay[p, q:q + 1, cols] + b_col * dec_inject[p, q:q + 1, cols]
                    y = jnp.where(row8 == q, jnp.sum(state * c_col, axis=0, keepdims=True), y)
                staged[2 * p + i, :, cols] = state
            value = (y + dec_skip[p, :, cols]) * dec_gate[p, :, cols]
            dec_gated[p, :, cols] = value
            at = pl.ds(pl.multiple_of(p * 8, 8), 8)
            dec_squares[at, :] = dec_squares[at, :] + value * value
            return 0

        lax.fori_loop(0, pairs, pair, 0)
        copy = pltpu.make_async_copy(
            staged.at[:, :, pl.ds(j * PART, PART)], state_hbm.at[:, :, pl.ds(j * PART, PART)],
            local_sem.at[blocks + 1 + j],
        )
        copy.start()
        state_out.append(copy)

    def summed(which, copies):
        for copy in copies:
            copy.wait_recv()
        acc = pack[which]
        for d in range(1, TENSORS):
            acc = acc + got[which, d]
        return lax.rsqrt(acc / CHAN + EPS)

    gain_row = gain[...]
    behind_by = 2
    pre_out = []
    for j in range(PARTS):
        forward(j)
        if j >= behind_by:
            decode(j - behind_by)
        if j == 3:
            scale = summed(0, pre_copies)
            lane_t = iota((8, 128), 1)
            req8 = row8 * 4 + lane_t // LEN
            scale = jnp.where(lax.rem(lane_t, LEN) < from_scalars(lengths, req8, REQ), scale, 0.0)
            for q in range(4):
                squares[q * 128:(q + 1) * 128, :] = jnp.transpose(
                    jnp.broadcast_to(scale[q:q + 1, :], (128, 128))
                )

            def finish(r, _):
                col = squares[pl.ds(pl.multiple_of(r * LEN, LEN), LEN), :]
                for p in range(WIDTH // 128):
                    at = slice(p * 128, (p + 1) * 128)
                    pre_v[r, :, at] = (mixed[r, :, at] * col * gain_row[:, at]).astype(BF16)
                return 0

            lax.fori_loop(0, REQ, finish, 0)
            copy = pltpu.make_async_copy(pre_v, pre_hbm, local_sem.at[blocks + 1 + PARTS])
            copy.start()
            pre_out.append(copy)
    for j in range(PARTS - behind_by, PARTS):
        decode(j)

    sums = jnp.sum(jnp.transpose(dec_squares[...]), axis=0, keepdims=True)
    pack[1] = jnp.broadcast_to(sums, (8, 128))
    dec_copies = exchange(1)
    scale = summed(1, dec_copies)
    column = jnp.transpose(jnp.broadcast_to(scale[0:1, :], (128, 128)))
    for p in range(pairs):
        col = column[p * 8:(p + 1) * 8, :]
        for c in range(WIDTH // 128):
            at = slice(c * 128, (c + 1) * 128)
            value = (dec_gated[p, :, at] * col * gain_row[:, at]).astype(BF16)
            dec_v[2 * p, :, at] = value[0:STEPS]
            dec_v[2 * p + 1, :, at] = value[STEPS:2 * STEPS]
    dec_copy = pltpu.make_async_copy(dec_v, dec_hbm, local_sem.at[blocks + 2 + PARTS])
    dec_copy.start()

    for j in range(PARTS):
        z_out[j].wait_send()
        group_copy(j, 1, GROUPS - 1).wait_send()
    for copy in pre_copies + dec_copies:
        copy.wait_send()
    for copy in state_out + pre_out:
        copy.wait()
    dec_copy.wait()


def local(
    x_pre, z_pre, b_pre, c_pre, dt_pre, lengths, owner,
    dec_x, dec_z, dec_b, dec_c, dec_dt, decay_rate, dt_bias, skip, norm_gain,
):
    smem = pl.BlockSpec(memory_space=pltpu.SMEM)
    vmem = pl.BlockSpec(memory_space=pltpu.VMEM)
    anywhere = pl.BlockSpec(memory_space=pl.ANY)
    tokens = (REQ, LEN, WIDTH)
    steps = (REQ // 2, 8, WIDTH)
    scratch = [
        pltpu.VMEM(tokens, BF16),
        pltpu.VMEM(tokens, BF16),
        pltpu.VMEM((REQ * HEADS, 128), F32),
        pltpu.VMEM((REQ, LEN + STATE, 3 * LEN), BF16),
        pltpu.VMEM((REQ, 2 * LEN, 256), BF16),
        pltpu.VMEM(tokens, F32),
        pltpu.VMEM((REQ * LEN, 128), F32),
        pltpu.VMEM((PARTS, REQ, STATE, PART), F32),
        pltpu.VMEM((PARTS, 2 * GROUPS, STATE, PART), F32),
        pltpu.VMEM((REQ, STATE, WIDTH), F32),
        pltpu.VMEM(tokens, BF16),
        pltpu.VMEM((REQ, STEPS, WIDTH), BF16),
        pltpu.VMEM(steps, F32),
        pltpu.VMEM(steps, F32),
        pltpu.VMEM(steps, F32),
        pltpu.VMEM(steps, F32),
        pltpu.VMEM((REQ // 2, 2 * STATE, WIDTH), F32),
        pltpu.VMEM(steps, F32),
        pltpu.VMEM((128, 128), F32),
        pltpu.VMEM((2, 8, 128), F32),
        pltpu.VMEM((2, TENSORS, 8, 128), F32),
        pltpu.SMEM((2 * GROUPS,), jnp.int32),
        pltpu.SMEM((REQ,), jnp.int32),
        pltpu.SemaphoreType.DMA((WIDTH // BLOCK + 3 + PARTS,)),
        pltpu.SemaphoreType.DMA((2, PARTS)),
        pltpu.SemaphoreType.DMA((2, PARTS)),
        pltpu.SemaphoreType.DMA((4, TENSORS)),
    ]
    scratch += [pltpu.VMEM((REQ, STATE, PART), F32) for _ in range(PARTS)]
    scratch += [pltpu.VMEM((2 * GROUPS, STATE, PART), F32) for _ in range(PARTS)]
    return pl.pallas_call(
        kernel,
        out_shape=(
            jax.ShapeDtypeStruct(tokens, BF16),
            jax.ShapeDtypeStruct((REQ, STEPS, WIDTH), BF16),
            jax.ShapeDtypeStruct((REQ, STATE, WIDTH), F32),
        ),
        in_specs=[smem] * 5 + [vmem] * 9 + [anywhere] * 2,
        out_specs=(anywhere, anywhere, anywhere),
        scratch_shapes=scratch,
        compiler_params=pltpu.CompilerParams(
            collective_id=0, has_side_effects=True, vmem_limit_bytes=56 << 20
        ),
    )(
        lengths, owner, decay_rate, dt_bias, skip,
        jnp.transpose(b_pre, (0, 2, 1)), jnp.transpose(c_pre, (0, 2, 1)), jnp.transpose(dt_pre, (0, 2, 1)),
        dec_x, dec_z, dec_b, dec_c, dec_dt, norm_gain.reshape(1, WIDTH),
        x_pre, z_pre,
    )


def solution(mesh):
    cell = ("section", "group")
    return jax.shard_map(
        local,
        mesh=mesh,
        in_specs=(
            P(cell, None, "tensor"), P(cell, None, "tensor"), P(cell, None, None), P(cell, None, None),
            P(cell, None, "tensor"), P(cell), P(), P(cell, None, "tensor"), P(cell, None, "tensor"),
            P(cell, None, None), P(cell, None, None), P(cell, None, "tensor"),
            P("tensor"), P("tensor"), P("tensor"), P("tensor"),
        ),
        out_specs=(P(cell, None, "tensor"),) * 3,
        check_vma=False,
    )
```

time: 160 us -> 79.1 us (0.49)
  Pallas kernels: 0 us -> 74.2 us
  blocking collectives: 42.3 us -> 0 us
  waiting for transfers between devices: 35.5 us -> 0 us
  local copies, waits for them, and re-layouts: 35.1 us -> 4.02 us
  other arithmetic: 20.2 us -> 0 us
  starting transfers between devices: 14.3 us -> 0 us
  matrix products: 10.2 us -> 0 us
    pallas_call x0 -> x1, Pallas kernels: none -> 74.2 us  [local(): pl.pallas_call(kernel, out_shape=(jax.ShapeDtypeStruct(tokens, BF16), jax...]
    psum x1 -> x0, blocking collectives: 42.3 us -> none  [local(): pre_total = lax.psum(pre_squares, 'tensor')]
    ppermute x1 -> x0, waiting for transfers between devices: 34 us -> none  [from_behind(): lax.ppermute(array, axis, [(i, (i + by) % size) for i in range(size)])]
    reshape x9 -> x0, local copies, waits for them, and re-layouts: 12.9 us -> none  [the longest x2 6.48 us: local(): x_heads = x_float.reshape(req_count, tok_slots, head_count, head_size)]
    dot_general x3 -> x0, matrix products: 10.2 us -> none  [the longest x1 5.08 us: local(): jnp.einsum('rtsh,rshp->rthp', weights, x_heads, precision=HIGH)]
    reduce_sum x7 -> x0, other arithmetic: 8.33 us -> none  [the longest x1 3.93 us: local(): jnp.sum(carry_state * dec_c[:, step_index].astype(jnp.float32)[:, :, None...]
    all_to_all x1 -> x0, starting transfers between devices: 7.78 us -> none  [local(): lax.all_to_all(send_buffer, 'group', split_axis=0, concat_axis=0, tiled=T...]
    ppermute x1 -> x0, starting transfers between devices: 6.5 us -> none  [from_behind(): lax.ppermute(array, axis, [(i, (i + by) % size) for i in range(size)])]
  transfers between devices with their start and end apart: 2 -> 0, of which waited for: 2 -> 0; matrix products, arithmetic and copies ran while one was open for 22% -> 0% of each run, Pallas kernels for 0% -> 0%
where the time goes in v1:
time: 79.1 us; the launch traced here: 78.9 us
  Pallas kernels  74.2 us (94%)
  local copies, waits for them, and re-layouts  4.02 us (5%)
    pallas_call x1, Pallas kernels, local(): pl.pallas_call(kernel, out_shape=(jax.ShapeDtypeStruct(tokens, BF16), jax...  74.2 us
    unnamed x7, local copies, waits for them, and re-layouts  4.02 us

profile of v1, /device:TPU:1, one launch (start us, length us, event | category | flops | bytes accessed | tf_op | source)
XLA Modules:
  0.0 78.9 jit_solution(8651853587032202458)
XLA Ops:
  0.6 74.2 %shard_map.175 = (bf16[16,32,1024]{2,1,0:T(8,128)(2,1)}, bf16[16,4,1024]{2,1,0:T(4,128)(2,1)}, f32[16,16,1024]{2,1,0:T(8,128)}) custom-call(s32[16]{0:T(128)} %lengths.1, s32[1024]{0:T(1024)} %owner.1, f32[16]{0:T(128)} %rate.1, f32[16]{0:T(128)} %bias.1, f32[16]{0:T(128)} %skip.1, bf16[16,16,32]{2,1,0:T(8,128)(2,1)} %bitcast.5, ...), custom_call_target="tpu_custom_call" | custom-call | tf_op jit(solution)/shard_map/pallas_call | solution.py:431
  74.9 0.0 copy-start.1
  74.9 0.0 copy-start
  74.9 2.4 %copy.22 = bf16[16,32,1024]{2,1,0:T(8,128)(2,1)} copy(bf16[16,32,1024]{2,1,0:T(8,128)(2,1)} %get-tuple-element.6) | data formatting | bytes 2097152
  77.3 0.0 copy-done.1
  77.3 0.7 copy.23
  78.0 0.0 copy-done
  78.0 1.0 %copy.24 = f32[16,16,1024]{2,1,0:T(8,128)} copy(f32[16,16,1024]{2,1,0:T(8,128)S(1)} %copy-done) | data formatting | bytes 2097152
Async XLA Ops:
  74.9 2.4 %copy-start.1 = (bf16[16,4,1024]{2,1,0:T(4,128)(2,1)S(1)}, bf16[16,4,1024]{2,1,0:T(4,128)(2,1)}, u32[]{:S(2)}) copy-start(bf16[16,4,1024]{2,1,0:T(4,128)(2,1)} %get-tuple-element.7) | copy-start | bytes 393220
  74.9 3.1 %copy-start = (f32[16,16,1024]{2,1,0:T(8,128)S(1)}, f32[16,16,1024]{2,1,0:T(8,128)}, u32[]{:S(2)}) copy-start(f32[16,16,1024]{2,1,0:T(8,128)} %get-tuple-element.8) | copy-start | bytes 3145732

commit v2 on v1

--- a/solution.py
+++ b/solution.py
@@ -26,6 +26,7 @@
 PARTS = 8
 PART = WIDTH // PARTS
 BLOCK = 256
+UNROLL = 8
 
 
 def iota(shape, dim):
@@ -132,9 +133,9 @@
         half = slice((r // half_reqs) * 128, (r // half_reqs) * 128 + 128)
         mine = lane128 == r % half_reqs
         for at, values in ((0, grow), (LEN, shrink)):
-            high, low = two_terms(jnp.where(mine, values[:, half], 0.0))
-            expand_lhs[r, at:at + LEN, 0:128] = high
-            expand_lhs[r, at:at + LEN, 128:256] = low
+            high, low = two_terms(values[:, r * HEADS:(r + 1) * HEADS])
+            expand_lhs[r, at:at + LEN, 0:HEADS] = high
+            expand_lhs[r, at:at + LEN, HEADS:2 * HEADS] = low
         gram = dot(jnp.where(mine, c_tok[:, half], 0.0).astype(BF16), b_rep[half].astype(BF16))
         high = gram.astype(BF16).astype(F32)
         lhs[r, 0:LEN, :] = jnp.where(causal, jnp.where(middle, gram - high, high), 0.0).astype(BF16)
@@ -143,18 +144,21 @@
         ).astype(BF16)
 
     z_out = []
-    for k in range(blocks):
+
+    def states(k):
         x_copies[k].wait()
         cols = slice(k * BLOCK, (k + 1) * BLOCK)
-        head_rows = lax.rem(iota((256, BLOCK), 0), HEADS)
-        head_cols = iota((256, BLOCK), 1) // 64 + k * (BLOCK // 64)
+        head_rows = lax.rem(iota((2 * HEADS, BLOCK), 0), HEADS)
+        head_cols = iota((2 * HEADS, BLOCK), 1) // 64 + k * (BLOCK // 64)
         expand = (head_rows == head_cols).astype(F32).astype(BF16)
         skip_row = from_scalars(skip, iota((1, BLOCK), 1) // 64 + k * (BLOCK // 64), HEADS)
 
-        def prefill(i, _, k=k, cols=cols, expand=expand, skip_row=skip_row):
-            for sub in range(4):
-                r = i * 4 + sub
-                wide = dot(expand_lhs[r], expand)
+        def prefill(i, _):
+            first = i * UNROLL
+            wides = dot(expand_lhs[pl.ds(first, UNROLL)].reshape(UNROLL * 2 * LEN, 2 * HEADS), expand)
+            for sub in range(UNROLL):
+                r = first + sub
+                wide = wides[sub * 2 * LEN:(sub + 1) * 2 * LEN]
                 x_f = x_v[r, :, cols].astype(F32)
                 high, low = two_terms(x_f * wide[0:LEN])
                 res = dot(lhs[r], jnp.concatenate([high, high, low], axis=0))
@@ -164,9 +168,9 @@
                     z_send[k * (BLOCK // PART) + p, r] = final[:, p * PART:(p + 1) * PART]
             return 0
 
-        lax.fori_loop(0, REQ // 4, prefill, 0)
-        if k == 0:
-            pl.semaphore_wait(barrier, 2 + (GROUPS - 1) + (TENSORS - 1))
+        lax.fori_loop(0, REQ // UNROLL, prefill, 0)
+
+    def send_on(k):
         for p in range(BLOCK // PART):
             j = k * (BLOCK // PART) + p
             copy = pltpu.make_async_remote_copy(
@@ -175,6 +179,72 @@
             )
             copy.start()
             z_out.append(copy)
+
+    states(0)
+    pl.semaphore_wait(barrier, 2 + (GROUPS - 1) + (TENSORS - 1))
+    send_on(0)
+    states(1)
+    send_on(1)
+
+    first_request = (behind * GROUPS + group) * REQ
+
+    def find_source(h, _):
+        low, high = jnp.int32(REQ - 1), jnp.int32(0)
+        for r in range(REQ):
+            is_it = owner[first_request + r] == h
+            low = jnp.minimum(low, jnp.where(is_it, r, REQ - 1))
+            high = jnp.maximum(high, jnp.where(is_it, r, 0))
+        source[2 * h] = low
+        source[2 * h + 1] = high
+        return 0
+
+    lax.fori_loop(0, GROUPS, find_source, 0)
+
+    def find_rows(cell, carry):
+        place, found = carry[0], carry[1:]
+        count = jnp.int32(0)
+        for r in range(REQ):
+            count = count + jnp.where(owner[(behind * GROUPS + cell) * REQ + r] == group, 1, 0)
+        has = jnp.where(count > 0, 1, 0)
+        spot = jnp.where(count > 0, place, -1)
+        return (place + has,) + tuple(jnp.where(spot == j, cell, v) for j, v in enumerate(found))
+
+    found = lax.fori_loop(0, GROUPS, find_rows, (jnp.int32(0),) * (1 + REQ // 2))[1:]
+    for j, cell in enumerate(found):
+        rows[2 * j] = 2 * cell
+        rows[2 * j + 1] = 2 * cell + 1
+
+    def group_copy(j, d, count=1):
+        rows_of = 2 * count
+        return pltpu.make_async_remote_copy(
+            x_send.at[j, pl.ds(2 * d, rows_of)],
+            x_recv[j].at[pl.ds(2 * group if count == 1 else 2 * d, rows_of)],
+            x_sem.at[0, j], x_sem.at[1, j],
+            device_id=(section, group_at(d), tensor), device_id_type=MESH,
+        )
+
+    def forward(j):
+        z_out[j].wait_recv()
+
+        for p in range(2):
+            x_recv[j][2 * group + p] = z_recv[j][source[2 * group + p]]
+
+        def fill(d, _):
+            h = group_at(d)
+            for p in range(2):
+                x_send[j, 2 * d + p] = z_recv[j][source[2 * h + p]]
+            group_copy(j, d).start()
+            return 0
+
+        lax.fori_loop(1, GROUPS, fill, 0)
+
+    forward(0)
+    states(2)
+    send_on(2)
+    forward(1)
+    states(3)
+    send_on(3)
+    forward(2)
 
     z_copy.wait()
 
@@ -241,58 +311,6 @@
         dec_cols[p] = dot(jnp.where(lane_p == p, cols_t, 0.0).astype(BF16), pick)
     dec_squares[...] = jnp.zeros_like(dec_squares)
 
-    first_request = (behind * GROUPS + group) * REQ
-
-    def find_source(h, _):
-        low, high = jnp.int32(REQ - 1), jnp.int32(0)
-        for r in range(REQ):
-            is_it = owner[first_request + r] == h
-            low = jnp.minimum(low, jnp.where(is_it, r, REQ - 1))
-            high = jnp.maximum(high, jnp.where(is_it, r, 0))
-        source[2 * h] = low
-        source[2 * h + 1] = high
-        return 0
-
-    lax.fori_loop(0, GROUPS, find_source, 0)
-
-    def find_rows(cell, carry):
-        place, found = carry[0], carry[1:]
-        count = jnp.int32(0)
-        for r in range(REQ):
-            count = count + jnp.where(owner[(behind * GROUPS + cell) * REQ + r] == group, 1, 0)
-        has = jnp.where(count > 0, 1, 0)
-        spot = jnp.where(count > 0, place, -1)
-        return (place + has,) + tuple(jnp.where(spot == j, cell, v) for j, v in enumerate(found))
-
-    found = lax.fori_loop(0, GROUPS, find_rows, (jnp.int32(0),) * (1 + REQ // 2))[1:]
-    for j, cell in enumerate(found):
-        rows[2 * j] = 2 * cell
-        rows[2 * j + 1] = 2 * cell + 1
-
-    def group_copy(j, d, count=1):
-        rows_of = 2 * count
-        return pltpu.make_async_remote_copy(
-            x_send.at[j, pl.ds(2 * d, rows_of)],
-            x_recv[j].at[pl.ds(2 * group if count == 1 else 2 * d, rows_of)],
-            x_sem.at[0, j], x_sem.at[1, j],
-            device_id=(section, group_at(d), tensor), device_id_type=MESH,
-        )
-
-    def forward(j):
-        z_out[j].wait_recv()
-
-        for p in range(2):
-            x_recv[j][2 * group + p] = z_recv[j][source[2 * group + p]]
-
-        def fill(d, _):
-            h = group_at(d)
-            for p in range(2):
-                x_send[j, 2 * d + p] = z_recv[j][source[2 * h + p]]
-            group_copy(j, d).start()
-            return 0
-
-        lax.fori_loop(1, GROUPS, fill, 0)
-
     state_out = []
 
     def decode(j):
@@ -333,34 +351,31 @@
         return lax.rsqrt(acc / CHAN + EPS)
 
     gain_row = gain[...]
-    behind_by = 2
     pre_out = []
-    for j in range(PARTS):
+    for j in range(3, PARTS):
         forward(j)
-        if j >= behind_by:
-            decode(j - behind_by)
-        if j == 3:
-            scale = summed(0, pre_copies)
-            lane_t = iota((8, 128), 1)
-            req8 = row8 * 4 + lane_t // LEN
-            scale = jnp.where(lax.rem(lane_t, LEN) < from_scalars(lengths, req8, REQ), scale, 0.0)
-            for q in range(4):
-                squares[q * 128:(q + 1) * 128, :] = jnp.transpose(
-                    jnp.broadcast_to(scale[q:q + 1, :], (128, 128))
-                )
-
-            def finish(r, _):
-                col = squares[pl.ds(pl.multiple_of(r * LEN, LEN), LEN), :]
-                for p in range(WIDTH // 128):
-                    at = slice(p * 128, (p + 1) * 128)
-                    pre_v[r, :, at] = (mixed[r, :, at] * col * gain_row[:, at]).astype(BF16)
-                return 0
-
-            lax.fori_loop(0, REQ, finish, 0)
-            copy = pltpu.make_async_copy(pre_v, pre_hbm, local_sem.at[blocks + 1 + PARTS])
-            copy.start()
-            pre_out.append(copy)
-    for j in range(PARTS - behind_by, PARTS):
+        decode(j - 3)
+    scale = summed(0, pre_copies)
+    lane_t = iota((8, 128), 1)
+    req8 = row8 * 4 + lane_t // LEN
+    scale = jnp.where(lax.rem(lane_t, LEN) < from_scalars(lengths, req8, REQ), scale, 0.0)
+    for q in range(4):
+        squares[q * 128:(q + 1) * 128, :] = jnp.transpose(
+            jnp.broadcast_to(scale[q:q + 1, :], (128, 128))
+        )
+
+    def finish(r, _):
+        col = squares[pl.ds(pl.multiple_of(r * LEN, LEN), LEN), :]
+        for p in range(WIDTH // 128):
+            at = slice(p * 128, (p + 1) * 128)
+            pre_v[r, :, at] = (mixed[r, :, at] * col * gain_row[:, at]).astype(BF16)
+        return 0
+
+    lax.fori_loop(0, REQ, finish, 0)
+    copy = pltpu.make_async_copy(pre_v, pre_hbm, local_sem.at[blocks + 1 + PARTS])
+    copy.start()
+    pre_out.append(copy)
+    for j in range(PARTS - 3, PARTS):
         decode(j)
 
     sums = jnp.sum(jnp.transpose(dec_squares[...]), axis=0, keepdims=True)
@@ -402,7 +417,7 @@
         pltpu.VMEM(tokens, BF16),
         pltpu.VMEM((REQ * HEADS, 128), F32),
         pltpu.VMEM((REQ, LEN + STATE, 3 * LEN), BF16),
-        pltpu.VMEM((REQ, 2 * LEN, 256), BF16),
+        pltpu.VMEM((REQ, 2 * LEN, 2 * HEADS), BF16),
         pltpu.VMEM(tokens, F32),
         pltpu.VMEM((REQ * LEN, 128), F32),
         pltpu.VMEM((PARTS, REQ, STATE, PART), F32),

time: 79.1 us -> 62.8 us (0.79)
  Pallas kernels: 74.2 us -> 57.9 us
    pallas_call x1, Pallas kernels: 74.2 us -> 57.9 us  [local(): pl.pallas_call(kernel, out_shape=(jax.ShapeDtypeStruct(tokens, BF16), jax...]
where the time goes in v2:
time: 62.8 us; the launch traced here: 62.6 us
  Pallas kernels  57.9 us (92%)
  local copies, waits for them, and re-layouts  4.02 us (6%)
  between operations  0.66 us (1%)
    pallas_call x1, Pallas kernels, local(): pl.pallas_call(kernel, out_shape=(jax.ShapeDtypeStruct(tokens, BF16), jax...  57.9 us
    unnamed x7, local copies, waits for them, and re-layouts  4.02 us

profile of v2, /device:TPU:1, one launch (start us, length us, event | category | flops | bytes accessed | tf_op | source)
XLA Modules:
  0.0 62.6 jit_solution(18292785894072969077)
XLA Ops:
  0.6 57.9 %shard_map.175 = (bf16[16,32,1024]{2,1,0:T(8,128)(2,1)}, bf16[16,4,1024]{2,1,0:T(4,128)(2,1)}, f32[16,16,1024]{2,1,0:T(8,128)}) custom-call(s32[16]{0:T(128)} %lengths.1, s32[1024]{0:T(1024)} %owner.1, f32[16]{0:T(128)} %rate.1, f32[16]{0:T(128)} %bias.1, f32[16]{0:T(128)} %skip.1, bf16[16,16,32]{2,1,0:T(8,128)(2,1)} %bitcast.5, ...), custom_call_target="tpu_custom_call" | custom-call | tf_op jit(solution)/shard_map/pallas_call | solution.py:446
  58.5 0.0 copy-start.1
  58.6 0.0 copy-start
  58.6 2.4 %copy.22 = bf16[16,32,1024]{2,1,0:T(8,128)(2,1)} copy(bf16[16,32,1024]{2,1,0:T(8,128)(2,1)} %get-tuple-element.6) | data formatting | bytes 2097152
  60.9 0.0 copy-done.1
  60.9 0.7 %copy.23 = bf16[16,4,1024]{2,1,0:T(4,128)(2,1)} copy(bf16[16,4,1024]{2,1,0:T(4,128)(2,1)S(1)} %copy-done.1) | data formatting | bytes 262144
  61.6 0.0 copy-done
  61.6 1.0 %copy.24 = f32[16,16,1024]{2,1,0:T(8,128)} copy(f32[16,16,1024]{2,1,0:T(8,128)S(1)} %copy-done) | data formatting | bytes 2097152
Async XLA Ops:
  58.5 2.4 %copy-start.1 = (bf16[16,4,1024]{2,1,0:T(4,128)(2,1)S(1)}, bf16[16,4,1024]{2,1,0:T(4,128)(2,1)}, u32[]{:S(2)}) copy-start(bf16[16,4,1024]{2,1,0:T(4,128)(2,1)} %get-tuple-element.7) | copy-start | bytes 393220
  58.6 3.1 %copy-start = (f32[16,16,1024]{2,1,0:T(8,128)S(1)}, f32[16,16,1024]{2,1,0:T(8,128)}, u32[]{:S(2)}) copy-start(f32[16,16,1024]{2,1,0:T(8,128)} %get-tuple-element.8) | copy-start | bytes 3145732

commit v3 on v2

--- a/solution.py
+++ b/solution.py
@@ -26,6 +26,8 @@
 PARTS = 8
 PART = WIDTH // PARTS
 BLOCK = 256
+GROUP_FIRST = (0, 1, 4, 5)
+PLACE_PARTS = 4
 UNROLL = 8
 
 
@@ -73,9 +75,9 @@
 ):
     (x_v, z_v, turn, lhs, expand_lhs, mixed, squares, z_send, x_send, staged, pre_v,
      dec_v, dec_decay, dec_inject, dec_skip, dec_gate, dec_cols, dec_gated, dec_squares,
-     pack, got, source, rows, local_sem, z_sem, x_sem, t_sem) = scratch[:27]
-    z_recv = scratch[27:27 + PARTS]
-    x_recv = scratch[27 + PARTS:27 + 2 * PARTS]
+     pack, got, source, rows, local_sem, z_sem, x_sem, t_sem, relay) = scratch[:28]
+    z_recv = scratch[28:28 + PARTS]
+    x_recv = scratch[28 + PARTS:28 + 2 * PARTS]
 
     section = lax.axis_index("section")
     group = lax.axis_index("group")
@@ -84,8 +86,12 @@
     ahead = lax.rem(section + 1, SECTIONS)
     behind = lax.rem(section + SECTIONS - 1, SECTIONS)
 
+    def farther_first(a):
+        return lax.rem(2 + a + a // 2 + 2 * (a // 3), SIDE)
+
     def group_at(d):
-        return lax.rem(gx + d // SIDE, SIDE) * SIDE + lax.rem(gy + lax.rem(d, SIDE), SIDE)
+        by_x, by_y = farther_first(d // SIDE), farther_first(lax.rem(d, SIDE))
+        return lax.rem(gx + by_x, SIDE) * SIDE + lax.rem(gy + by_y, SIDE)
 
     blocks = WIDTH // BLOCK
     x_copies = []
@@ -100,12 +106,14 @@
     barrier = pltpu.get_barrier_semaphore()
     for to in (ahead, behind):
         pl.semaphore_signal(barrier, inc=1, device_id=(to, group, tensor), device_id_type=MESH)
-    for d in range(1, GROUPS):
+    for d in range(GROUPS - 1):
         pl.semaphore_signal(barrier, inc=1, device_id=(section, group_at(d), tensor), device_id_type=MESH)
-    for d in range(1, TENSORS):
-        pl.semaphore_signal(
-            barrier, inc=1, device_id=(section, group, lax.rem(tensor + d, TENSORS)), device_id_type=MESH
-        )
+    core = lax.rem(tensor, 2)
+    near = [tensor + 1 - 2 * core]
+    for by in (2, TENSORS - 2):
+        near += [lax.rem(tensor - core + by, TENSORS) + c for c in range(2)]
+    for to in near:
+        pl.semaphore_signal(barrier, inc=1, device_id=(section, group, to), device_id_type=MESH)
 
     turn[...] = jnp.zeros_like(turn)
     turn[:, 0:LEN] = dt_t[...].reshape(REQ * HEADS, LEN)
@@ -143,8 +151,6 @@
             middle[0:STATE], 0.0, b_rep[r * STATE:(r + 1) * STATE]
         ).astype(BF16)
 
-    z_out = []
-
     def states(k):
         x_copies[k].wait()
         cols = slice(k * BLOCK, (k + 1) * BLOCK)
@@ -170,49 +176,40 @@
 
         lax.fori_loop(0, REQ // UNROLL, prefill, 0)
 
-    def send_on(k):
-        for p in range(BLOCK // PART):
-            j = k * (BLOCK // PART) + p
-            copy = pltpu.make_async_remote_copy(
-                z_send.at[j], z_recv[j], z_sem.at[0, j], z_sem.at[1, j],
-                device_id=(ahead, group, tensor), device_id_type=MESH,
-            )
-            copy.start()
-            z_out.append(copy)
-
-    states(0)
-    pl.semaphore_wait(barrier, 2 + (GROUPS - 1) + (TENSORS - 1))
-    send_on(0)
-    states(1)
-    send_on(1)
-
-    first_request = (behind * GROUPS + group) * REQ
-
-    def find_source(h, _):
-        low, high = jnp.int32(REQ - 1), jnp.int32(0)
-        for r in range(REQ):
-            is_it = owner[first_request + r] == h
-            low = jnp.minimum(low, jnp.where(is_it, r, REQ - 1))
-            high = jnp.maximum(high, jnp.where(is_it, r, 0))
-        source[2 * h] = low
-        source[2 * h + 1] = high
-        return 0
-
-    lax.fori_loop(0, GROUPS, find_source, 0)
-
-    def find_rows(cell, carry):
-        place, found = carry[0], carry[1:]
-        count = jnp.int32(0)
-        for r in range(REQ):
-            count = count + jnp.where(owner[(behind * GROUPS + cell) * REQ + r] == group, 1, 0)
-        has = jnp.where(count > 0, 1, 0)
-        spot = jnp.where(count > 0, place, -1)
-        return (place + has,) + tuple(jnp.where(spot == j, cell, v) for j, v in enumerate(found))
-
-    found = lax.fori_loop(0, GROUPS, find_rows, (jnp.int32(0),) * (1 + REQ // 2))[1:]
-    for j, cell in enumerate(found):
-        rows[2 * j] = 2 * cell
-        rows[2 * j + 1] = 2 * cell + 1
+    def section_copy(j):
+        return pltpu.make_async_remote_copy(
+            z_send.at[j], z_recv[j], z_sem.at[0, j], z_sem.at[1, j],
+            device_id=(ahead, group, tensor), device_id_type=MESH,
+        )
+
+    def find(at, from_section):
+        first_request = (from_section * GROUPS + group) * REQ
+
+        def find_source(h, _):
+            low, high = jnp.int32(REQ - 1), jnp.int32(0)
+            for r in range(REQ):
+                is_it = owner[first_request + r] == h
+                low = jnp.minimum(low, jnp.where(is_it, r, REQ - 1))
+                high = jnp.maximum(high, jnp.where(is_it, r, 0))
+            source[at, 2 * h] = low
+            source[at, 2 * h + 1] = high
+            return 0
+
+        def find_rows(cell, carry):
+            place, found = carry[0], carry[1:]
+            count = jnp.int32(0)
+            for r in range(REQ):
+                is_it = owner[(from_section * GROUPS + cell) * REQ + r] == group
+                count = count + jnp.where(is_it, 1, 0)
+            has = jnp.where(count > 0, 1, 0)
+            spot = jnp.where(count > 0, place, -1)
+            return (place + has,) + tuple(jnp.where(spot == j, cell, v) for j, v in enumerate(found))
+
+        lax.fori_loop(0, GROUPS, find_source, 0)
+        found = lax.fori_loop(0, GROUPS, find_rows, (jnp.int32(0),) * (1 + REQ // 2))[1:]
+        for j, cell in enumerate(found):
+            rows[at, 2 * j] = 2 * cell
+            rows[at, 2 * j + 1] = 2 * cell + 1
 
     def group_copy(j, d, count=1):
         rows_of = 2 * count
@@ -223,28 +220,52 @@
             device_id=(section, group_at(d), tensor), device_id_type=MESH,
         )
 
-    def forward(j):
-        z_out[j].wait_recv()
-
+    def to_groups(j, state_of, at):
         for p in range(2):
-            x_recv[j][2 * group + p] = z_recv[j][source[2 * group + p]]
+            x_recv[j][2 * group + p] = state_of(source[at, 2 * group + p])
 
         def fill(d, _):
             h = group_at(d)
             for p in range(2):
-                x_send[j, 2 * d + p] = z_recv[j][source[2 * h + p]]
+                x_send[j, 2 * d + p] = state_of(source[at, 2 * h + p])
             group_copy(j, d).start()
             return 0
 
-        lax.fori_loop(1, GROUPS, fill, 0)
-
-    forward(0)
+        lax.fori_loop(0, GROUPS - 1, fill, 0)
+
+    def group_second(j):
+        section_copy(j).wait_recv()
+        to_groups(j, lambda r: z_recv[j][r], 0)
+
+    def group_first(j):
+        to_groups(j, lambda r: z_send[j, r], 1)
+
+    def section_second(j):
+        group_copy(j, 0, GROUPS - 1).wait_recv()
+        for k in range(REQ):
+            z_send[j, k] = x_recv[j][rows[1, k]]
+        section_copy(j).start()
+
+    find(1, section)
+    states(0)
+    states(1)
+    pl.semaphore_wait(barrier, 2 + (GROUPS - 1) + len(near))
+    pl.semaphore_signal(
+        relay, inc=1, device_id=(section, group, lax.rem(tensor + 2, TENSORS)), device_id_type=MESH
+    )
+    section_copy(2).start()
+    group_first(0)
+    section_copy(3).start()
+    group_first(1)
     states(2)
-    send_on(2)
-    forward(1)
+    group_first(4)
+    group_first(5)
     states(3)
-    send_on(3)
-    forward(2)
+    section_copy(6).start()
+    section_copy(7).start()
+    find(0, behind)
+    group_second(2)
+    section_second(0)
 
     z_copy.wait()
 
@@ -278,6 +299,7 @@
         sums = jnp.sum(jnp.transpose(squares[q * 128:(q + 1) * 128, :]), axis=0, keepdims=True)
         packed = jnp.where(row8 == q, sums, packed)
     pack[0] = packed
+    pl.semaphore_wait(relay, 1)
     pre_copies = exchange(0)
 
     turn[...] = jnp.zeros_like(turn)
@@ -314,13 +336,19 @@
     state_out = []
 
     def decode(j):
-        group_copy(j, 1, GROUPS - 1).wait_recv()
+        if j in GROUP_FIRST:
+            section_copy(j).wait_recv()
+        else:
+            group_copy(j, 0, GROUPS - 1).wait_recv()
         cols = slice(j * PART, (j + 1) * PART)
 
         def pair(p, _):
             y = jnp.zeros((8, PART), F32)
             for i in range(2):
-                state = x_recv[j][rows[2 * p + i]]
+                if j in GROUP_FIRST:
+                    state = z_recv[j][2 * p + i]
+                else:
+                    state = x_recv[j][rows[0, 2 * p + i]]
                 for t in range(STEPS):
                     q = i * STEPS + t
                     b_col = dec_cols[p, 0:STATE, q * 128:(q + 1) * 128]
@@ -352,9 +380,17 @@
 
     gain_row = gain[...]
     pre_out = []
-    for j in range(3, PARTS):
-        forward(j)
-        decode(j - 3)
+    group_second(3)
+    section_second(1)
+    group_second(6)
+    section_second(4)
+    group_second(7)
+    section_second(5)
+    decode(0)
+    decode(2)
+    decode(1)
+    decode(3)
+    decode(4)
     scale = summed(0, pre_copies)
     lane_t = iota((8, 128), 1)
     req8 = row8 * 4 + lane_t // LEN
@@ -375,8 +411,9 @@
     copy = pltpu.make_async_copy(pre_v, pre_hbm, local_sem.at[blocks + 1 + PARTS])
     copy.start()
     pre_out.append(copy)
-    for j in range(PARTS - 3, PARTS):
-        decode(j)
+    decode(6)
+    decode(5)
+    decode(7)
 
     sums = jnp.sum(jnp.transpose(dec_squares[...]), axis=0, keepdims=True)
     pack[1] = jnp.broadcast_to(sums, (8, 128))
@@ -394,13 +431,30 @@
     dec_copy.start()
 
     for j in range(PARTS):
-        z_out[j].wait_send()
-        group_copy(j, 1, GROUPS - 1).wait_send()
+        section_copy(j).wait_send()
+        group_copy(j, 0, GROUPS - 1).wait_send()
     for copy in pre_copies + dec_copies:
         copy.wait_send()
     for copy in state_out + pre_out:
         copy.wait()
     dec_copy.wait()
+
+
+def place(pre, dec, state, pre_hbm, dec_hbm, state_hbm, pre_v, dec_v, state_v, in_sem, out_sem):
+    parts = [(dec, dec_v, dec_hbm)]
+    for k in range(PLACE_PARTS):
+        some = pl.ds(k * (REQ // PLACE_PARTS), REQ // PLACE_PARTS)
+        parts.append((pre.at[some], pre_v.at[some], pre_hbm.at[some]))
+        parts.append((state.at[some], state_v.at[some], state_hbm.at[some]))
+    arriving = [pltpu.make_async_copy(a, b, in_sem.at[k]) for k, (a, b, _) in enumerate(parts)]
+    leaving = [pltpu.make_async_copy(b, c, out_sem.at[k]) for k, (_, b, c) in enumerate(parts)]
+    for copy in arriving:
+        copy.start()
+    for copy, then in zip(arriving, leaving):
+        copy.wait()
+        then.start()
+    for copy in leaving:
+        copy.wait()
 
 
 def local(
@@ -434,16 +488,17 @@
         pltpu.VMEM((128, 128), F32),
         pltpu.VMEM((2, 8, 128), F32),
         pltpu.VMEM((2, TENSORS, 8, 128), F32),
-        pltpu.SMEM((2 * GROUPS,), jnp.int32),
-        pltpu.SMEM((REQ,), jnp.int32),
+        pltpu.SMEM((2, 2 * GROUPS), jnp.int32),
+        pltpu.SMEM((2, REQ), jnp.int32),
         pltpu.SemaphoreType.DMA((WIDTH // BLOCK + 3 + PARTS,)),
         pltpu.SemaphoreType.DMA((2, PARTS)),
         pltpu.SemaphoreType.DMA((2, PARTS)),
         pltpu.SemaphoreType.DMA((4, TENSORS)),
+        pltpu.SemaphoreType.REGULAR,
     ]
     scratch += [pltpu.VMEM((REQ, STATE, PART), F32) for _ in range(PARTS)]
     scratch += [pltpu.VMEM((2 * GROUPS, STATE, PART), F32) for _ in range(PARTS)]
-    return pl.pallas_call(
+    outs = pl.pallas_call(
         kernel,
         out_shape=(
             jax.ShapeDtypeStruct(tokens, BF16),
@@ -462,6 +517,16 @@
         dec_x, dec_z, dec_b, dec_c, dec_dt, norm_gain.reshape(1, WIDTH),
         x_pre, z_pre,
     )
+    return pl.pallas_call(
+        place,
+        out_shape=tuple(jax.ShapeDtypeStruct(v.shape, v.dtype) for v in outs),
+        in_specs=[anywhere] * 3,
+        out_specs=(anywhere,) * 3,
+        scratch_shapes=[pltpu.VMEM(v.shape, v.dtype) for v in outs] + [
+            pltpu.SemaphoreType.DMA((2 * PLACE_PARTS + 1,)) for _ in range(2)
+        ],
+        compiler_params=pltpu.CompilerParams(vmem_limit_bytes=56 << 20),
+    )(*outs)
 
 
 def solution(mesh):

time: 62.8 us -> 56.1 us (0.89)
  local copies, waits for them, and re-layouts: 4.02 us -> 0 us
  Pallas kernels: 57.9 us -> 55.3 us
    pallas_call x1, Pallas kernels: 57.9 us -> 52.8 us  [local(): pl.pallas_call(kernel, out_shape=(jax.ShapeDtypeStruct(tokens, BF16), jax...]
    unnamed x7 -> x0, local copies, waits for them, and re-layouts: 4.02 us -> none
    pallas_call x0 -> x1, Pallas kernels: none -> 2.48 us  [local(): pl.pallas_call(place, out_shape=tuple((jax.ShapeDtypeStruct(v.shape, v.dt...]
where the time goes in v3:
time: 56.1 us; the launch traced here: 56 us
  Pallas kernels  55.3 us (99%)
  between operations  0.65 us (1%)
    pallas_call x1, Pallas kernels, local(): pl.pallas_call(kernel, out_shape=(jax.ShapeDtypeStruct(tokens, BF16), jax...  52.8 us
    pallas_call x1, Pallas kernels, local(): pl.pallas_call(place, out_shape=tuple((jax.ShapeDtypeStruct(v.shape, v.dt...  2.48 us

profile of v3, /device:TPU:1, one launch (start us, length us, event | category | flops | bytes accessed | tf_op | source)
XLA Modules:
  0.0 56.0 jit_solution(11337724871141000611)
XLA Ops:
  0.6 52.8 %shard_map.175 = (bf16[16,32,1024]{2,1,0:T(8,128)(2,1)}, bf16[16,4,1024]{2,1,0:T(4,128)(2,1)}, f32[16,16,1024]{2,1,0:T(8,128)}) custom-call(s32[16]{0:T(128)} %lengths.1, s32[1024]{0:T(1024)} %owner.1, f32[16]{0:T(128)} %rate.1, f32[16]{0:T(128)} %bias.1, f32[16]{0:T(128)} %skip.1, bf16[16,16,32]{2,1,0:T(8,128)(2,1)} %bitcast.5, ...), custom_call_target="tpu_custom_call" | custom-call | tf_op jit(solution)/shard_map/pallas_call | solution.py:501
  53.5 2.5 %shard_map.176 = (bf16[16,32,1024]{2,1,0:T(8,128)(2,1)}, bf16[16,4,1024]{2,1,0:T(4,128)(2,1)}, f32[16,16,1024]{2,1,0:T(8,128)}) custom-call(bf16[16,32,1024]{2,1,0:T(8,128)(2,1)} %get-tuple-element.6.pre, bf16[16,4,1024]{2,1,0:T(4,128)(2,1)} %get-tuple-element.7.dec, f32[16,16,1024]{2,1,0:T(8,128)} %get-tuple-element.8.state), custom_call_target="tpu_custom_call" | custom-call | tf_op jit(solution)/shard_map/pallas_call | solution.py:520

commit v4 on v3

--- a/solution.py
+++ b/solution.py
@@ -283,9 +283,10 @@
 
     def exchange(which):
         copies = []
+        used = 4 if which == 0 else 1
         for d in range(1, TENSORS):
             copy = pltpu.make_async_remote_copy(
-                pack.at[which], got.at[which, d], t_sem.at[2 * which, d], t_sem.at[2 * which + 1, d],
+                pack.at[which, pl.ds(0, used)], got.at[which, d, pl.ds(0, used)], t_sem.at[2 * which, d], t_sem.at[2 * which + 1, d],
                 device_id=(section, group, lax.rem(tensor + d, TENSORS)), device_id_type=MESH,
             )
             copy.start()
@@ -374,8 +375,10 @@
         for copy in copies:
             copy.wait_recv()
         acc = pack[which]
+        used = 4 if which == 0 else 1
+        acc = acc[0:used]
         for d in range(1, TENSORS):
-            acc = acc + got[which, d]
+            acc = acc + got[which, d, 0:used]
         return lax.rsqrt(acc / CHAN + EPS)
 
     gain_row = gain[...]
@@ -392,8 +395,8 @@
     decode(3)
     decode(4)
     scale = summed(0, pre_copies)
-    lane_t = iota((8, 128), 1)
-    req8 = row8 * 4 + lane_t // LEN
+    lane_t = iota((4, 128), 1)
+    req8 = iota((4, 128), 0) * 4 + lane_t // LEN
     scale = jnp.where(lax.rem(lane_t, LEN) < from_scalars(lengths, req8, REQ), scale, 0.0)
     for q in range(4):
         squares[q * 128:(q + 1) * 128, :] = jnp.transpose(
@@ -419,7 +422,7 @@
     pack[1] = jnp.broadcast_to(sums, (8, 128))
     dec_copies = exchange(1)
     scale = summed(1, dec_copies)
-    column = jnp.transpose(jnp.broadcast_to(scale[0:1, :], (128, 128)))
+    column = jnp.transpose(jnp.broadcast_to(scale, (128, 128)))
     for p in range(pairs):
         col = column[p * 8:(p + 1) * 8, :]
         for c in range(WIDTH // 128):

time: 56.1 us -> 55.7 us (level)
  no operation moved by 1% of the time
where the time goes in v4:
time: 55.7 us; the launch traced here: 55.5 us
  Pallas kernels  54.9 us (99%)
  between operations  0.65 us (1%)
    pallas_call x1, Pallas kernels, local(): pl.pallas_call(kernel, out_shape=(jax.ShapeDtypeStruct(tokens, BF16), jax...  52.4 us
    pallas_call x1, Pallas kernels, local(): pl.pallas_call(place, out_shape=tuple((jax.ShapeDtypeStruct(v.shape, v.dt...  2.48 us

profile of v4, /device:TPU:1, one launch (start us, length us, event | category | flops | bytes accessed | tf_op | source)
XLA Modules:
  0.0 55.5 jit_solution(15564655876151877140)
XLA Ops:
  0.6 52.4 %shard_map.175 = (bf16[16,32,1024]{2,1,0:T(8,128)(2,1)}, bf16[16,4,1024]{2,1,0:T(4,128)(2,1)}, f32[16,16,1024]{2,1,0:T(8,128)}) custom-call(s32[16]{0:T(128)} %lengths.1, s32[1024]{0:T(1024)} %owner.1, f32[16]{0:T(128)} %rate.1, f32[16]{0:T(128)} %bias.1, f32[16]{0:T(128)} %skip.1, bf16[16,16,32]{2,1,0:T(8,128)(2,1)} %bitcast.5, ...), custom_call_target="tpu_custom_call" | custom-call | tf_op jit(solution)/shard_map/pallas_call | solution.py:504
  53.0 2.5 %shard_map.176 = (bf16[16,32,1024]{2,1,0:T(8,128)(2,1)}, bf16[16,4,1024]{2,1,0:T(4,128)(2,1)}, f32[16,16,1024]{2,1,0:T(8,128)}) custom-call(bf16[16,32,1024]{2,1,0:T(8,128)(2,1)} %get-tuple-element.6.pre, bf16[16,4,1024]{2,1,0:T(4,128)(2,1)} %get-tuple-element.7.dec, f32[16,16,1024]{2,1,0:T(8,128)} %get-tuple-element.8.state), custom_call_target="tpu_custom_call" | custom-call | tf_op jit(solution)/shard_map/pallas_call | solution.py:523

commit v5 on v4

--- a/solution.py
+++ b/solution.py
@@ -248,15 +248,15 @@
 
     find(1, section)
     states(0)
-    states(1)
     pl.semaphore_wait(barrier, 2 + (GROUPS - 1) + len(near))
     pl.semaphore_signal(
         relay, inc=1, device_id=(section, group, lax.rem(tensor + 2, TENSORS)), device_id_type=MESH
     )
+    group_first(0)
+    group_first(1)
+    states(1)
     section_copy(2).start()
-    group_first(0)
     section_copy(3).start()
-    group_first(1)
     states(2)
     group_first(4)
     group_first(5)

time: 55.7 us -> 56.6 us (1.016)
  Pallas kernels: 54.9 us -> 55.8 us
    pallas_call x1, Pallas kernels: 52.4 us -> 53.3 us  [local(): pl.pallas_call(kernel, out_shape=(jax.ShapeDtypeStruct(tokens, BF16), jax...]
where the time goes in v5:
time: 56.6 us; the launch traced here: 56.5 us
  Pallas kernels  55.8 us (99%)
  between operations  0.65 us (1%)
    pallas_call x1, Pallas kernels, local(): pl.pallas_call(kernel, out_shape=(jax.ShapeDtypeStruct(tokens, BF16), jax...  53.3 us
    pallas_call x1, Pallas kernels, local(): pl.pallas_call(place, out_shape=tuple((jax.ShapeDtypeStruct(v.shape, v.dt...  2.48 us

profile of v5, /device:TPU:1, one launch (start us, length us, event | category | flops | bytes accessed | tf_op | source)
XLA Modules:
  0.0 56.5 jit_solution(3699700878931160907)
XLA Ops:
  0.6 53.3 %shard_map.175 = (bf16[16,32,1024]{2,1,0:T(8,128)(2,1)}, bf16[16,4,1024]{2,1,0:T(4,128)(2,1)}, f32[16,16,1024]{2,1,0:T(8,128)}) custom-call(s32[16]{0:T(128)} %lengths.1, s32[1024]{0:T(1024)} %owner.1, f32[16]{0:T(128)} %rate.1, f32[16]{0:T(128)} %bias.1, f32[16]{0:T(128)} %skip.1, bf16[16,16,32]{2,1,0:T(8,128)(2,1)} %bitcast.5, ...), custom_call_target="tpu_custom_call" | custom-call | tf_op jit(solution)/shard_map/pallas_call | solution.py:504
  54.0 2.5 %shard_map.176 = (bf16[16,32,1024]{2,1,0:T(8,128)(2,1)}, bf16[16,4,1024]{2,1,0:T(4,128)(2,1)}, f32[16,16,1024]{2,1,0:T(8,128)}) custom-call(bf16[16,32,1024]{2,1,0:T(8,128)(2,1)} %get-tuple-element.6.pre, bf16[16,4,1024]{2,1,0:T(4,128)(2,1)} %get-tuple-element.7.dec, f32[16,16,1024]{2,1,0:T(8,128)} %get-tuple-element.8.state), custom_call_target="tpu_custom_call" | custom-call | tf_op jit(solution)/shard_map/pallas_call | solution.py:523
